TPU v7x, 32 devices: a whole 2x2x4 slice. The times are simulated.
32 devices in a mesh: seq: 16 (over z, y, core), blk: 2 (over x).
Axes of the slice: x: 2, y: 2, z: 4, core: 2. Of those that a mesh axis runs over, the one named last changes fastest.
Arguments:
- tokens: bfloat16 [32, 1024, 768], P('seq', 'blk'), may hold values from -6 to 6
- sent_lengths: int32 [32, 4], P('seq'), may hold values from 0 to 1024, as said below
- w_query: bfloat16 [768, 768], P('seq'), may hold values from -0.21875 to 0.21875
- w_key: bfloat16 [768, 768], P('seq'), may hold values from -0.21875 to 0.21875
- w_value: bfloat16 [768, 768], P('seq'), may hold values from -0.21875 to 0.21875
- w_out: bfloat16 [768, 768], P('seq'), may hold values from -1.75 to 1.75
- shared_a: bfloat16 [768, 1024], P('seq'), may hold values from -0.21875 to 0.21875
- shared_b: bfloat16 [1024, 768], P('seq'), may hold values from -0.1875 to 0.1875
- w_in: bfloat16 [768, 3072], P('seq'), may hold values from -0.21875 to 0.21875
- w_back: bfloat16 [3072, 768], P('seq'), may hold values from -0.109375 to 0.109375
- gain_one: float32 [768], replicated, may hold values from 0.5 to 1.5
- gain_two: float32 [768], replicated, may hold values from 0.5 to 1.5
- scale_dq: float32 [1024], replicated, may hold values from 0.5 to 2
- shift_bq: float32 [768], replicated, may hold values from -4 to 4
- scale_dv: float32 [1024], replicated, may hold values from 0.5 to 2
- shift_bv: float32 [768], replicated, may hold values from -4 to 4
- cotangent: bfloat16 [32, 1024, 768], P('seq', 'blk'), may hold values from -6 to 6
Outputs:
- layer_out: bfloat16 [32, 1024, 768], P('seq', 'blk')
- grad_tokens: bfloat16 [32, 1024, 768], P('seq', 'blk')
- grad_dq: float32 [1024], replicated
- grad_bq: float32 [768], replicated
- grad_dv: float32 [1024], replicated
- grad_bv: float32 [768], replicated
Inputs may be any that keep to these rules, and one draw needn't show every extreme that they name: `sent_lengths`: rows come in groups of 2 (the rows of one index of seq). In each group one row holds a single document of 1024 tokens and empty other slots. Every other row holds two to four sentences in order and then padding: the first two have 8 to 512 tokens each, the third and fourth 0 to 1024 // 2 (the fourth empty when the third is), and all together at most 1024 tokens.
All inputs are finite; a program needn't handle non-finite values.
Results may differ from a plain program's by a relative error of at most 0.024.
Values may be sent and summed in bfloat16 or wider, within the bound.
No kernel may reach another device: no remote copies, remote signals or barrier semaphores. Data moves between devices by JAX's collectives and lax.ppermute only.
A program may use at most 192 MiB of HBM per device.

v0:
```python
import jax
import jax.numpy as jnp
from jax import lax
from jax.sharding import PartitionSpec as P

HEADS = 12
HEAD_DIM = 64


def shifted(shard, axis, by):
    count = lax.axis_size(axis)
    return lax.ppermute(shard, axis, [(i, (i + by) % count) for i in range(count)])


def layer_norm(hidden, gain):
    centre = hidden - jnp.mean(hidden, axis=-1, keepdims=True)
    spread = jnp.mean(centre * centre, axis=-1, keepdims=True)
    return centre * lax.rsqrt(spread + 1e-05) * gain


def exact_gelu(values):
    return jax.nn.gelu(values, approximate=False)


def segment_ids(lengths, total):
    place = jnp.arange(total, dtype=jnp.int32)[None, :]
    bounds = jnp.cumsum(lengths, axis=1)
    counted = jnp.zeros((lengths.shape[0], total), jnp.int32)
    for column in range(lengths.shape[1]):
        counted = counted + (place >= bounds[:, column : column + 1]).astype(jnp.int32)
    return counted


def dot_plain(left, right):
    return jnp.dot(left, right, preferred_element_type=jnp.float32)


def dot_trans(left, right):
    return lax.dot_general(
        left, right, (((1,), (1,)), ((), ())), preferred_element_type=jnp.float32
    )


def block_grads(query_h, out_grad, lse_rows, delta_rows, key_h, value_h, allowed):
    scores = (
        jnp.einsum("rqhd,rkhd->rqhk", query_h, key_h, preferred_element_type=jnp.float32) * 0.125
    )
    probs = jnp.where(allowed, jnp.exp(scores - lse_rows[..., None]), 0.0)
    value_grad = jnp.einsum(
        "rqhk,rqhd->rkhd", probs.astype(jnp.bfloat16), out_grad, preferred_element_type=jnp.float32
    )
    prob_grad = jnp.einsum("rqhd,rkhd->rqhk", out_grad, value_h, preferred_element_type=jnp.float32)
    score_grad = (probs * (prob_grad - delta_rows[..., None])).astype(jnp.bfloat16)
    query_grad = (
        jnp.einsum("rqhk,rkhd->rqhd", score_grad, key_h, preferred_element_type=jnp.float32) * 0.125
    )
    key_grad = (
        jnp.einsum("rqhk,rqhd->rkhd", score_grad, query_h, preferred_element_type=jnp.float32)
        * 0.125
    )
    return (query_grad, key_grad, value_grad)


def body(
    tokens,
    sent_lengths,
    w_query,
    w_key,
    w_value,
    w_out,
    shared_a,
    shared_b,
    w_in,
    w_back,
    gain_one,
    gain_two,
    scale_dq,
    shift_bq,
    scale_dv,
    shift_bv,
    cotangent,
):
    row_count, span, width = tokens.shape
    head_count = HEADS
    head_size = HEAD_DIM
    blocks = lax.axis_size("blk")
    my_block = lax.axis_index("blk")
    token_count = row_count * span
    token_rows = tokens.reshape(token_count, width)
    seg_full = segment_ids(sent_lengths, span * blocks)
    seg_mine = lax.dynamic_slice_in_dim(seg_full, my_block * span, span, 1)
    w_queries, w_keys, w_values, proj_a, proj_b = (
        lax.all_gather(w_query, "seq", axis=0, tiled=True),
        lax.all_gather(w_key, "seq", axis=0, tiled=True),
        lax.all_gather(w_value, "seq", axis=0, tiled=True),
        lax.all_gather(shared_a, "seq", axis=0, tiled=True),
        lax.all_gather(shared_b, "seq", axis=0, tiled=True),
    )
    projected = dot_plain(token_rows, proj_a).astype(jnp.bfloat16)
    proj_float = projected.astype(jnp.float32)
    lift_q = (proj_float * scale_dq).astype(jnp.bfloat16)
    lift_v = (proj_float * scale_dv).astype(jnp.bfloat16)
    extra_q = dot_plain(lift_q, proj_b)
    extra_v = dot_plain(lift_v, proj_b)
    queries = (dot_plain(token_rows, w_queries) + shift_bq * extra_q).astype(jnp.bfloat16)
    key_rows = dot_plain(token_rows, w_keys).astype(jnp.bfloat16)
    value_rows = (dot_plain(token_rows, w_values) + shift_bv * extra_v).astype(jnp.bfloat16)
    shape4 = (row_count, span, head_count, head_size)
    query_h = queries.reshape(shape4)
    key_h = key_rows.reshape(shape4)
    value_h = value_rows.reshape(shape4)
    start_best = jnp.full((row_count, span, head_count), -1e30, jnp.float32)
    best = start_best
    key_piece = lax.all_gather(key_rows.reshape(row_count, span, width), "blk", axis=1, tiled=True)
    value_piece = lax.all_gather(
        value_rows.reshape(row_count, span, width), "blk", axis=1, tiled=True
    )
    length = key_piece.shape[1]
    key_part = key_piece.reshape(row_count, length, head_count, head_size)
    value_part = value_piece.reshape(row_count, length, head_count, head_size)
    seg_keys = seg_full
    allowed = (seg_mine[:, :, None] == seg_keys[:, None, :])[:, :, None, :]
    scores = (
        jnp.einsum("rqhd,rkhd->rqhk", query_h, key_part, preferred_element_type=jnp.float32) * 0.125
    )
    scores = jnp.where(allowed, scores, -1e30)
    new_best = jnp.maximum(best, jnp.max(scores, axis=-1))
    weight = jnp.where(allowed, jnp.exp(scores - new_best[..., None]), 0.0)
    total = jnp.sum(weight, axis=-1)
    accum = jnp.einsum(
        "rqhk,rkhd->rqhd",
        weight.astype(jnp.bfloat16),
        value_part,
        preferred_element_type=jnp.float32,
    )
    best, total, accum = (new_best, total, accum)
    log_total = best + jnp.log(total)
    context = accum / total[..., None]
    context_b = context.reshape(token_count, width).astype(jnp.bfloat16)
    w_outs, w_ins, w_backs = (
        lax.all_gather(w_out, "seq", axis=0, tiled=True),
        lax.all_gather(w_in, "seq", axis=0, tiled=True),
        lax.all_gather(w_back, "seq", axis=0, tiled=True),
    )

    def norm_first(hidden):
        return layer_norm(hidden, gain_one)

    def norm_second(hidden):
        return layer_norm(hidden, gain_two)

    resid_one = token_rows.astype(jnp.float32) + dot_plain(context_b, w_outs)
    normed_one, norm_one_pull = jax.vjp(norm_first, resid_one)
    pre_act = dot_plain(normed_one.astype(jnp.bfloat16), w_ins)
    act_float, gelu_pull = jax.vjp(exact_gelu, pre_act)
    ffn_part = dot_plain(act_float.astype(jnp.bfloat16), w_backs)
    normed_two, norm_two_pull = jax.vjp(norm_second, normed_one + ffn_part)
    layer_out = normed_two.astype(jnp.bfloat16).reshape(row_count, span, width)
    w_outs, w_ins, w_backs = (
        lax.all_gather(w_out, "seq", axis=0, tiled=True),
        lax.all_gather(w_in, "seq", axis=0, tiled=True),
        lax.all_gather(w_back, "seq", axis=0, tiled=True),
    )
    (grad_two,) = norm_two_pull(cotangent.reshape(token_count, width).astype(jnp.float32))
    act_grad = dot_trans(grad_two.astype(jnp.bfloat16), w_backs)
    (pre_grad,) = gelu_pull(act_grad)
    normed_grad = grad_two + dot_trans(pre_grad.astype(jnp.bfloat16), w_ins)
    (grad_one,) = norm_one_pull(normed_grad)
    context_grad = dot_trans(grad_one.astype(jnp.bfloat16), w_outs).astype(jnp.bfloat16)
    out_grad = context_grad.reshape(shape4)
    delta_rows = jnp.sum(out_grad.astype(jnp.float32) * context, axis=-1)
    zero_grads = jnp.zeros(shape4, jnp.float32)

    def key_step(step, carry):
        key_cur, value_cur, query_acc, key_acc, value_acc = carry
        source = (my_block - step) % blocks
        seg_keys = lax.dynamic_slice_in_dim(seg_full, source * span, span, 1)
        allowed = (seg_mine[:, :, None] == seg_keys[:, None, :])[:, :, None, :]
        q_part, k_part, v_part = block_grads(
            query_h, out_grad, log_total, delta_rows, key_cur, value_cur, allowed
        )
        key_acc, value_acc = (
            shifted((key_acc + k_part).astype(jnp.bfloat16), "blk", 1).astype(jnp.float32),
            shifted((value_acc + v_part).astype(jnp.bfloat16), "blk", 1).astype(jnp.float32),
        )
        key_cur, value_cur = shifted((key_cur, value_cur), "blk", 1)
        return (key_cur, value_cur, query_acc + q_part, key_acc, value_acc)

    looped = lax.fori_loop(
        0, blocks, key_step, (key_h, value_h, zero_grads, zero_grads, zero_grads)
    )
    query_acc, key_acc, value_acc = (looped[2], looped[3], looped[4])
    query_grad = query_acc.reshape(token_count, width).astype(jnp.bfloat16)
    key_grad = key_acc.reshape(token_count, width).astype(jnp.bfloat16)
    value_grad = value_acc.reshape(token_count, width).astype(jnp.bfloat16)
    w_queries, w_keys, w_values, proj_a, proj_b = (
        lax.all_gather(w_query, "seq", axis=0, tiled=True),
        lax.all_gather(w_key, "seq", axis=0, tiled=True),
        lax.all_gather(w_value, "seq", axis=0, tiled=True),
        lax.all_gather(shared_a, "seq", axis=0, tiled=True),
        lax.all_gather(shared_b, "seq", axis=0, tiled=True),
    )
    query_float = query_grad.astype(jnp.float32)
    value_float = value_grad.astype(jnp.float32)
    part_bq = jnp.sum(query_float * extra_q, axis=0)
    part_bv = jnp.sum(value_float * extra_v, axis=0)
    lift_q_grad = dot_trans((query_float * shift_bq).astype(jnp.bfloat16), proj_b)
    lift_v_grad = dot_trans((value_float * shift_bv).astype(jnp.bfloat16), proj_b)
    part_dq = jnp.sum(lift_q_grad * proj_float, axis=0)
    part_dv = jnp.sum(lift_v_grad * proj_float, axis=0)
    proj_grad = (lift_q_grad * scale_dq + lift_v_grad * scale_dv).astype(jnp.bfloat16)
    token_grad = (
        grad_one
        + dot_trans(query_grad, w_queries)
        + dot_trans(key_grad, w_keys)
        + dot_trans(value_grad, w_values)
        + dot_trans(proj_grad, proj_a)
    )
    grad_dq, grad_bq, grad_dv, grad_bv = lax.psum(
        (part_dq, part_bq, part_dv, part_bv), ("seq", "blk")
    )
    return (
        layer_out,
        token_grad.astype(jnp.bfloat16).reshape(row_count, span, width),
        grad_dq,
        grad_bq,
        grad_dv,
        grad_bv,
    )


def solution(mesh):
    return jax.shard_map(
        body,
        mesh=mesh,
        in_specs=(
            P("seq", "blk", None),
            P("seq", None),
            P("seq", None),
            P("seq", None),
            P("seq", None),
            P("seq", None),
            P("seq", None),
            P("seq", None),
            P("seq", None),
            P("seq", None),
            P(),
            P(),
            P(),
            P(),
            P(),
            P(),
            P("seq", "blk", None),
        ),
        out_specs=(P("seq", "blk", None), P("seq", "blk", None), P(), P(), P(), P()),
        check_vma=False,
    )
```

profile of v0, /device:TPU:0, one launch (start us, length us, event | category | flops | bytes accessed | tf_op | source)
XLA Modules:
  0.0 946.6 jit_solution(6786457126780168972)
XLA Ops:
  10.6 40.8 %all-gather.19.cloned.1.call-done = bf16[768,768]{1,0:T(8,128)(2,1)} async-done(((bf16[48,768]{1,0:T(8,128)(2,1)}), bf16[768,768]{1,0:T(8,128)(2,1)}) %all-gather.19.cloned.1.call-update) | async-done | bytes 1179664 | tf_op jit(solution)/shard_map/all_gather | solution.py:94
  55.8 36.5 %all-gather.13.cloned.1.call-done = bf16[768,1024]{1,0:T(8,128)(2,1)} async-done(((bf16[48,1024]{1,0:T(8,128)(2,1)}), bf16[768,1024]{1,0:T(8,128)(2,1)}) %all-gather.13.cloned.1.call-update) | async-done | bytes 1572880 | tf_op jit(solution)/shard_map/all_gather | solution.py:96
  96.8 36.4 %all-gather.15.cloned.1.call-done = bf16[1024,768]{1,0:T(8,128)(2,1)} async-done(((bf16[64,768]{1,0:T(8,128)(2,1)}), bf16[1024,768]{1,0:T(8,128)(2,1)}) %all-gather.15.cloned.1.call-update) | async-done | bytes 1572880 | tf_op jit(solution)/shard_map/all_gather | solution.py:97
  137.0 35.5 %all-gather.11.cloned.1.call-done = bf16[768,768]{1,0:T(8,128)(2,1)} async-done(((bf16[48,768]{1,0:T(8,128)(2,1)}), bf16[768,768]{1,0:T(8,128)(2,1)}) %all-gather.11.cloned.1.call-update) | async-done | bytes 1179664 | tf_op jit(solution)/shard_map/all_gather | solution.py:95
  197.2 14.9 %all-gather.23.cloned.1.call-done = bf16[768,768]{1,0:T(8,128)(2,1)} async-done(((bf16[48,768]{1,0:T(8,128)(2,1)}), bf16[768,768]{1,0:T(8,128)(2,1)}) %all-gather.23.cloned.1.call-update) | async-done | bytes 1179664 | tf_op jit(solution)/shard_map/all_gather | solution.py:93
  229.1 28.9 %all-gather.21.cloned.1.call-done = bf16[2,1024,768]{2,1,0:T(8,128)(2,1)} async-done(((bf16[2,512,768]{2,1,0:T(8,128)(2,1)}), bf16[2,1024,768]{2,1,0:T(8,128)(2,1)}) %all-gather.21.cloned.1.call-update) | async-done | bytes 3145744 | tf_op jit(solution)/shard_map/all_gather | solution.py:114
  262.6 20.3 %fusion.14 = (f32[2,512,12]{1,2,0:T(8,128)S(1)}, f32[2,12,1024,512]{3,2,1,0:T(8,128)}) fusion(pred[2,512,1024]{1,2,0:T(8,128)(4,1)S(1)} %broadcast_compare_fusion.1, bf16[2,1024,12,64]{1,3,2,0:T(8,128)(2,1)} %bitcast.159, bf16[2,512,12,64]{1,0,3,2:T(2,128)(2,1)S(1)} %reshape.205), kind=kOutput, calls=%fused_computation.20 | convolution fusion | flops 1648349184 | bytes 56147968 | tf_op jit(solution)/shard_map/rqhd,rkhd->rqhk/dot_general | solution.py:124
  283.0 21.6 %fusion.15 = f32[2,512,12]{1,2,0:T(8,128)S(1)} fusion(f32[2,12,1024,512]{3,2,1,0:T(8,128)} %get-tuple-element.434, f32[2,512,12]{1,2,0:T(8,128)S(1)} %broadcast_maximum_fusion, pred[2,512,1024]{1,2,0:T(8,128)(4,1)S(1)} %broadcast_compare_fusion.1), kind=kLoop, calls=%fused_computation.21 | loop fusion | flops 62902272 | bytes 51478528 | tf_op jit(solution)/shard_map/reduce_sum | solution.py:129
  310.0 22.7 %fusion.83 = (bf16[2,512,12,64]{1,3,2,0:T(8,128)(2,1)S(1)}, f32[2,512,12,64]{1,3,2,0:T(8,128)}) fusion(f32[2,512,12]{1,2,0:T(8,128)S(1)} %fusion.15, bf16[2,1024,12,64]{1,3,2,0:T(8,128)(2,1)} %bitcast.168, f32[2,12,1024,512]{3,2,1,0:T(8,128)} %get-tuple-element.434, f32[2,512,12]{1,2,0:T(8,128)S(1)} %broadcast_maximum_fusion, ...), kind=kOutput, calls=%fused_computation.141 | convolution fusion | flops 1675100160 | bytes 59342848 | tf_op jit(solution)/shard_map/rqhk,rkhd->rqhd/dot_general | solution.py:130
  349.4 50.4 %all-gather.27.cloned.1.call-done = bf16[768,3072]{1,0:T(8,128)(2,1)} async-done(((bf16[48,3072]{1,0:T(8,128)(2,1)}), bf16[768,3072]{1,0:T(8,128)(2,1)}) %all-gather.27.cloned.1.call-update) | async-done | bytes 4718608 | tf_op jit(solution)/shard_map/all_gather | solution.py:142
  399.8 36.2 %fusion.20 = (f32[1024,3072]{1,0:T(8,128)}, f32[1024,3072]{1,0:T(8,128)}) fusion(bf16[768,3072]{1,0:T(8,128)(2,1)} %all-gather.27.cloned.1.call-done, f32[1024,768]{1,0:T(8,128)S(1)} %get-tuple-element.438, f32[768]{0:T(1024)S(1)} %copy-done.40, f32[1024]{0:T(1024)S(1)} %fusion.70, f32[1024]{0:T(1024)S(1)} %broadcast_multiply_fusion.1), kind=kOutput, calls=%fused_computation.26 | convolution fusion | flops 5030019072 | bytes 33041408 | tf_op jit(solution)/shard_map/dot_general | solution.py:35
  436.0 17.9 %all-gather.29.cloned.1.call-done = bf16[3072,768]{1,0:T(8,128)(2,1)} async-done(((bf16[192,768]{1,0:T(8,128)(2,1)}), bf16[3072,768]{1,0:T(8,128)(2,1)}) %all-gather.29.cloned.1.call-update) | async-done | bytes 4718608 | tf_op jit(solution)/shard_map/all_gather | solution.py:143
  470.5 22.1 %multiply_reduce_fusion.1 = (f32[1024]{0:T(1024)S(1)}, f32[1024,768]{1,0:T(8,128)}) fusion(f32[1024,768]{1,0:T(8,128)S(1)} %get-tuple-element.438, f32[1024]{0:T(1024)S(1)} %broadcast_multiply_fusion.1, f32[768]{0:T(1024)S(1)} %copy-done.40, bf16[768,3072]{1,0:T(8,128)(2,1)} %all-gather.27.cloned.1.call-done, f32[1024,3072]{1,0:T(8,128)} %get-tuple-element.439, ...), kind=kOutput, calls=%fused_computation.71 | convolution fusion | flops 9714007040 | bytes 44055552 | tf_op jit(solution)/shard_map/dot_general | solution.py:39
  503.6 358.2 %while.24 = (s32[]{:T(128)}, bf16[2,512,12,64]{1,3,2,0:T(8,128)(2,1)}, bf16[2,512,12,64]{1,3,2,0:T(8,128)(2,1)}, f32[2,512,12,64]{1,3,2,0:T(8,128)}, f32[2,512,1...) while((s32[]{:T(128)}, ...), condition=%wide.region_13.14_spmd.clone, body=%wide.region_12.13_spmd.clone.sunk | while | flops 4099407872 | bytes 182616576 | solution.py:189
  519.1 15.8 %fusion.155 = bf16[2,512,12,512]{1,3,2,0:T(8,128)(2,1)} fusion(f32[2,12,512,512]{3,2,1,0:T(8,128)} %fusion.154, f32[2,512,12]{1,2,0:T(8,128)S(1)} %get-tuple-element.575, f32[2,512,12]{1,2,0:T(8,128)S(1)} %get-tuple-element.573, pred[2,512,512]{1,2,0:T(8,128)(4,1)} %broadcast_compare_fusion.3, bf16[2,512,12,64]{1,3,2,0:T(8,128)(2,1)} %copy.78, ...), kind=kOutput, calls=%fused_computation.2.clone.1 | convolution fusion | flops 843055104 | bytes 41517056 | tf_op jit(solution)/shard_map/while/body/eval_jaxpr/rqhd,rkhd->rqhk/dot_general | solution.py:52
  585.6 30.1 %collective-permute-done.3 = bf16[2,512,12,64]{1,3,2,0:T(8,128)(2,1)} collective-permute-done((bf16[2,512,12,64]{1,3,2,0:T(8,128)(2,1)}, bf16[2,512,12,64]{1,3,2,0:T(8,128)(2,1)}, u32[]{:S(2)}, u32[]{:S(2)}) %collective-permute-start.3) | collective-permute-done | bytes 1572896 | tf_op jit(solution)/shard_map/while/body/eval_jaxpr/ppermute | solution.py:12
  619.3 30.2 %collective-permute-done = bf16[2,512,12,64]{1,3,2,0:T(8,128)(2,1)} collective-permute-done((bf16[2,512,12,64]{1,3,2,0:T(8,128)(2,1)S(1)}, bf16[2,512,12,64]{1,3,2,0:T(8,128)(2,1)}, u32[]{:S(2)}, u32[]{:S(2)}) %collective-permute-start) | collective-permute-done | bytes 1572896 | tf_op jit(solution)/shard_map/while/body/eval_jaxpr/ppermute | solution.py:12
  649.5 33.0 %collective-permute-done.1 = bf16[2,512,12,64]{1,3,2,0:T(8,128)(2,1)} collective-permute-done((bf16[2,512,12,64]{1,3,2,0:T(8,128)(2,1)}, bf16[2,512,12,64]{1,3,2,0:T(8,128)(2,1)}, u32[]{:S(2)}, u32[]{:S(2)}) %collective-permute-start.1) | collective-permute-done | bytes 1572896 | tf_op jit(solution)/shard_map/while/body/eval_jaxpr/ppermute | solution.py:12
  697.9 15.8 %fusion.155 = bf16[2,512,12,512]{1,3,2,0:T(8,128)(2,1)} fusion(f32[2,12,512,512]{3,2,1,0:T(8,128)} %fusion.154, f32[2,512,12]{1,2,0:T(8,128)S(1)} %get-tuple-element.575, f32[2,512,12]{1,2,0:T(8,128)S(1)} %get-tuple-element.573, pred[2,512,512]{1,2,0:T(8,128)(4,1)} %broadcast_compare_fusion.3, bf16[2,512,12,64]{1,3,2,0:T(8,128)(2,1)} %copy.78, ...), kind=kOutput, calls=%fused_computation.2.clone.1 | convolution fusion | flops 843055104 | bytes 41517056 | tf_op jit(solution)/shard_map/while/body/eval_jaxpr/rqhd,rkhd->rqhk/dot_general | solution.py:52
  725.8 13.4 %fusion.157 = bf16[2,512,12,64]{1,3,2,0:T(8,128)(2,1)} fusion(f32[2,512,12,64]{1,3,2,0:T(8,128)} %get-tuple-element.550, bf16[2,512,12,64]{1,3,2,0:T(8,128)(2,1)} %get-tuple-element.574, f32[2,12,512,512]{3,2,1,0:T(8,128)} %fusion.154, f32[2,512,12]{1,2,0:T(8,128)S(1)} %get-tuple-element.573, pred[2,512,512]{1,2,0:T(8,128)(4,1)} %broadcast_compare_fusion.3, ...), kind=kOutput, calls=%fused_computation.10.clone.1 | convolution fusion | flops 832831488 | bytes 32030720 | tf_op jit(solution)/shard_map/while/body/eval_jaxpr/rqhk,rqhd->rkhd/dot_general | solution.py:49
  765.5 30.1 %collective-permute-done.3 = bf16[2,512,12,64]{1,3,2,0:T(8,128)(2,1)} collective-permute-done((bf16[2,512,12,64]{1,3,2,0:T(8,128)(2,1)}, bf16[2,512,12,64]{1,3,2,0:T(8,128)(2,1)}, u32[]{:S(2)}, u32[]{:S(2)}) %collective-permute-start.3) | collective-permute-done | bytes 1572896 | tf_op jit(solution)/shard_map/while/body/eval_jaxpr/ppermute | solution.py:12
  799.2 30.2 %collective-permute-done = bf16[2,512,12,64]{1,3,2,0:T(8,128)(2,1)} collective-permute-done((bf16[2,512,12,64]{1,3,2,0:T(8,128)(2,1)S(1)}, bf16[2,512,12,64]{1,3,2,0:T(8,128)(2,1)}, u32[]{:S(2)}, u32[]{:S(2)}) %collective-permute-start) | collective-permute-done | bytes 1572896 | tf_op jit(solution)/shard_map/while/body/eval_jaxpr/ppermute | solution.py:12
  829.3 32.1 %collective-permute-done.1 = bf16[2,512,12,64]{1,3,2,0:T(8,128)(2,1)} collective-permute-done((bf16[2,512,12,64]{1,3,2,0:T(8,128)(2,1)}, bf16[2,512,12,64]{1,3,2,0:T(8,128)(2,1)}, u32[]{:S(2)}, u32[]{:S(2)}) %collective-permute-start.1) | collective-permute-done | bytes 1572896 | tf_op jit(solution)/shard_map/while/body/eval_jaxpr/ppermute | solution.py:12
  886.7 39.6 %all-reduce = (f32[1024]{0:T(1024)}, f32[768]{0:T(1024)}, f32[1024]{0:T(1024)}, f32[768]{0:T(1024)}) all-reduce(f32[1024]{0:T(1024)S(1)} %get-tuple-element.391, f32[768]{0:T(1024)S(1)} %get-tuple-element.446, f32[1024]{0:T(1024)S(1)} %get-tuple-element.390, ...), channel_id=1, replica_groups=mesh['seq'=16,'blk'=2] {'seq','blk'}, use_global_device_ids=true, to_apply=%region_15.16 | all-reduce | flops 3584 | bytes 28672 | tf_op jit(solution)/shard_map/psum | solution.py:219
  (202 shorter events, 276.7 us)
Async XLA Ops:
  7.2 44.2 %all-gather.19.cloned.1.call-start = ((), (), s32[]{:S(2)}) async-start(), calls=%async_computation.4 | async-start | bytes 1253376 | tf_op jit(solution)/shard_map/all_gather | solution.py:94
  7.9 84.4 %all-gather.13.cloned.1.call-start = ((), (), s32[]{:S(2)}) async-start(), calls=%async_computation.1 | async-start | bytes 1671168 | tf_op jit(solution)/shard_map/all_gather | solution.py:96
  8.6 124.5 %all-gather.15.cloned.1.call-start = ((), (), s32[]{:S(2)}) async-start(), calls=%async_computation.2 | async-start | bytes 1671168 | tf_op jit(solution)/shard_map/all_gather | solution.py:97
  9.4 163.2 %all-gather.11.cloned.1.call-start = ((), (), s32[]{:S(2)}) async-start(), calls=%async_computation | async-start | bytes 1253376 | tf_op jit(solution)/shard_map/all_gather | solution.py:95
  10.0 202.1 %all-gather.23.cloned.1.call-start = ((), (), s32[]{:S(2)}) async-start(), calls=%async_computation.6 | async-start | bytes 1253376 | tf_op jit(solution)/shard_map/all_gather | solution.py:93
  10.5 247.4 %all-gather.21.cloned.1.call-start = ((), (), s32[]{:S(2)}) async-start(), calls=%async_computation.5 | async-start | bytes 4718592 | tf_op jit(solution)/shard_map/all_gather | solution.py:114
  51.3 40.9 %copy-start.37 = (bf16[2,512,768]{2,1,0:T(8,128)(2,1)S(1)}, bf16[2,512,768]{2,1,0:T(8,128)(2,1)}, u32[]{:S(2)}) copy-start(bf16[2,512,768]{2,1,0:T(8,128)(2,1)} %param.19) | copy-start | bytes 4718596
  55.8 77.4 %copy-start.32 = (f32[1024]{0:T(1024)S(1)}, f32[1024]{0:T(1024)}, u32[]{:S(2)}) copy-start(f32[1024]{0:T(1024)} %param.33) | copy-start | bytes 12292
  55.8 249.5 %all-gather.17.cloned.1.call-start = ((), (), s32[]{:S(2)}) async-start(), calls=%async_computation.3 | async-start | bytes 4718592 | tf_op jit(solution)/shard_map/all_gather | solution.py:115
  96.8 75.8 %copy-start.30 = (f32[768]{0:T(1024)S(1)}, f32[768]{0:T(1024)}, u32[]{:S(2)}) copy-start(f32[768]{0:T(1024)} %param.34) | copy-start | bytes 9220
  137.0 42.0 %copy-start.36 = (s32[2,4]{1,0:T(2,128)S(1)}, s32[2,4]{1,0:T(2,128)}, u32[]{:S(2)}) copy-start(s32[2,4]{1,0:T(2,128)} %param.20) | copy-start | bytes 100
  176.9 168.2 %all-gather.25.cloned.1.call-start = ((), (), s32[]{:S(2)}) async-start(), calls=%async_computation.7 | async-start | bytes 1253376 | tf_op jit(solution)/shard_map/all_gather | solution.py:141
  177.7 222.1 %all-gather.27.cloned.1.call-start = ((), (), s32[]{:S(2)}) async-start(), calls=%async_computation.8 | async-start | bytes 5013504 | tf_op jit(solution)/shard_map/all_gather | solution.py:142
  178.4 275.5 %all-gather.29.cloned.1.call-start = ((), (), s32[]{:S(2)}) async-start(), calls=%async_computation.9 | async-start | bytes 5013504 | tf_op jit(solution)/shard_map/all_gather | solution.py:143
  348.9 50.9 %copy-start.40 = (f32[768]{0:T(1024)S(1)}, f32[768]{0:T(1024)}, u32[]{:S(2)}) copy-start(f32[768]{0:T(1024)} %param.29) | copy-start | bytes 9220
  544.5 37.5 %collective-permute-start.2 = (bf16[2,512,12,64]{1,3,2,0:T(8,128)(2,1)}, bf16[2,512,12,64]{1,3,2,0:T(8,128)(2,1)}, u32[]{:S(2)}, u32[]{:S(2)}) collective-permute-start(bf16[2,512,12,64]{1,3,2,0:T(8,128)(2,1)} %fusion.156), channel_id=1, source_target_pairs={{0,1},{1,0},{2,3},{3,2},{4,5},{5,4},{6,7},{7,6},{8,9},{9,8},{10,11... | collective-permute-start | bytes 4718600 | tf_op jit(solution)/shard_map/while/body/eval_jaxpr/ppermute | solution.py:12
  558.4 57.4 %collective-permute-start.3 = (bf16[2,512,12,64]{1,3,2,0:T(8,128)(2,1)}, bf16[2,512,12,64]{1,3,2,0:T(8,128)(2,1)}, u32[]{:S(2)}, u32[]{:S(2)}) collective-permute-start(bf16[2,512,12,64]{1,3,2,0:T(8,128)(2,1)} %fusion.157), channel_id=1, source_target_pairs={{0,1},{1,0},{2,3},{3,2},{4,5},{5,4},{6,7},{7,6},{8,9},{9,8},{10,11... | collective-permute-start | bytes 4718600 | tf_op jit(solution)/shard_map/while/body/eval_jaxpr/ppermute | solution.py:12
  558.9 90.5 %collective-permute-start = (bf16[2,512,12,64]{1,3,2,0:T(8,128)(2,1)S(1)}, bf16[2,512,12,64]{1,3,2,0:T(8,128)(2,1)}, u32[]{:S(2)}, u32[]{:S(2)}) collective-permute-start(bf16[2,512,12,64]{1,3,2,0:T(8,128)(2,1)S(1)} %copy.77), channel_id=1, source_target_pairs={{0,1},{1,0},{2,3},{3,2},{4,5},{5,4},{6,7},{7,6},{8,9},{9,8},{10,11... | collective-permute-start | bytes 4718600 | tf_op jit(solution)/shard_map/while/body/eval_jaxpr/ppermute | solution.py:12
  560.4 122.1 %collective-permute-start.1 = (bf16[2,512,12,64]{1,3,2,0:T(8,128)(2,1)}, bf16[2,512,12,64]{1,3,2,0:T(8,128)(2,1)}, u32[]{:S(2)}, u32[]{:S(2)}) collective-permute-start(bf16[2,512,12,64]{1,3,2,0:T(8,128)(2,1)} %copy.78), channel_id=1, source_target_pairs={{0,1},{1,0},{2,3},{3,2},{4,5},{5,4},{6,7},{7,6},{8,9},{9,8},{10,11... | collective-permute-start | bytes 4718600 | tf_op jit(solution)/shard_map/while/body/eval_jaxpr/ppermute | solution.py:12
  724.3 37.6 %collective-permute-start.2 = (bf16[2,512,12,64]{1,3,2,0:T(8,128)(2,1)}, bf16[2,512,12,64]{1,3,2,0:T(8,128)(2,1)}, u32[]{:S(2)}, u32[]{:S(2)}) collective-permute-start(bf16[2,512,12,64]{1,3,2,0:T(8,128)(2,1)} %fusion.156), channel_id=1, source_target_pairs={{0,1},{1,0},{2,3},{3,2},{4,5},{5,4},{6,7},{7,6},{8,9},{9,8},{10,11... | collective-permute-start | bytes 4718600 | tf_op jit(solution)/shard_map/while/body/eval_jaxpr/ppermute | solution.py:12
  739.1 56.5 %collective-permute-start.3 = (bf16[2,512,12,64]{1,3,2,0:T(8,128)(2,1)}, bf16[2,512,12,64]{1,3,2,0:T(8,128)(2,1)}, u32[]{:S(2)}, u32[]{:S(2)}) collective-permute-start(bf16[2,512,12,64]{1,3,2,0:T(8,128)(2,1)} %fusion.157), channel_id=1, source_target_pairs={{0,1},{1,0},{2,3},{3,2},{4,5},{5,4},{6,7},{7,6},{8,9},{9,8},{10,11... | collective-permute-start | bytes 4718600 | tf_op jit(solution)/shard_map/while/body/eval_jaxpr/ppermute | solution.py:12
  739.7 89.7 %collective-permute-start = (bf16[2,512,12,64]{1,3,2,0:T(8,128)(2,1)S(1)}, bf16[2,512,12,64]{1,3,2,0:T(8,128)(2,1)}, u32[]{:S(2)}, u32[]{:S(2)}) collective-permute-start(bf16[2,512,12,64]{1,3,2,0:T(8,128)(2,1)S(1)} %copy.77), channel_id=1, source_target_pairs={{0,1},{1,0},{2,3},{3,2},{4,5},{5,4},{6,7},{7,6},{8,9},{9,8},{10,11... | collective-permute-start | bytes 4718600 | tf_op jit(solution)/shard_map/while/body/eval_jaxpr/ppermute | solution.py:12
  741.1 120.3 %collective-permute-start.1 = (bf16[2,512,12,64]{1,3,2,0:T(8,128)(2,1)}, bf16[2,512,12,64]{1,3,2,0:T(8,128)(2,1)}, u32[]{:S(2)}, u32[]{:S(2)}) collective-permute-start(bf16[2,512,12,64]{1,3,2,0:T(8,128)(2,1)} %copy.78), channel_id=1, source_target_pairs={{0,1},{1,0},{2,3},{3,2},{4,5},{5,4},{6,7},{7,6},{8,9},{9,8},{10,11... | collective-permute-start | bytes 4718600 | tf_op jit(solution)/shard_map/while/body/eval_jaxpr/ppermute | solution.py:12
  882.7 43.5 %copy-start.12 = (bf16[96,8,2,512]{3,1,2,0:T(8,128)(2,1)S(1)}, bf16[96,8,2,512]{3,1,2,0:T(8,128)(2,1)}, u32[]{:S(2)}) copy-start(bf16[96,8,2,512]{3,1,2,0:T(8,128)(2,1)} %copy-done.11) | copy-start | bytes 4718596
  (37 other events, 171.0 us)
Sparse Core Ops, SparseCore 0:
  10.3 41.0 all-gather.18
  53.6 38.6 all-gather.12
  94.6 38.5 all-gather.14
  135.3 37.2 all-gather.10
  174.7 37.2 all-gather.22
  214.0 43.8 all-gather.20
  259.5 44.9 all-gather.16
  306.7 38.3 all-gather.24
  347.4 52.3 all-gather.26
  401.9 51.9 all-gather.28
where the time goes:
time: 952 us; the launch traced here: 947 us
  waiting for transfers between devices  484 us (51%)
  matrix products  278 us (29%)
  local copies, waits for them, and re-layouts  67.2 us (7%)
  other arithmetic  52.9 us (6%)
  blocking collectives  39.6 us (4%)
  between operations  14.9 us (2%)
    ppermute x8, waiting for transfers between devices, shifted(): lax.ppermute(shard, axis, [(i, (i + by) % count) for i in range(count)])  209 us
    dot_general x9, matrix products, dot_plain(): return jnp.dot(left, right, preferred_element_type=jnp.float32)  79.2 us
    all_gather x1, waiting for transfers between devices, body(): lax.all_gather(w_in, 'seq', axis=0, tiled=True)  50.4 us
    all_gather x1, waiting for transfers between devices, body(): lax.all_gather(w_key, 'seq', axis=0, tiled=True)  40.8 us
    dot_general x8, matrix products, dot_trans(): lax.dot_general(left, right, (((1,), (1,)), ((), ())), preferred_element_...  40.4 us
    psum x1, blocking collectives, body(): lax.psum((part_dq, part_bq, part_dv, part_bv), ('seq', 'blk'))  39.6 us
    all_gather x1, waiting for transfers between devices, body(): lax.all_gather(shared_a, 'seq', axis=0, tiled=True)  36.5 us
    all_gather x1, waiting for transfers between devices, body(): lax.all_gather(shared_b, 'seq', axis=0, tiled=True)  36.4 us
  transfers between devices with their start and end apart: 18, of which 17 were waited for; matrix products, arithmetic and copies ran while one was open for 24% of the time, Pallas kernels for 0%

commit v1 on v0

--- a/solution.py
+++ b/solution.py
@@ -1,10 +1,354 @@
+import functools
+import math
+
 import jax
 import jax.numpy as jnp
 from jax import lax
+from jax.experimental import pallas as pl
+from jax.experimental.pallas import tpu as pltpu
 from jax.sharding import PartitionSpec as P
 
 HEADS = 12
 HEAD_DIM = 64
+bf16 = jnp.bfloat16
+f32 = jnp.float32
+
+
+LN2 = 0.6931471805599453
+LOG2E = 1.4426950408889634
+SEGS = 5
+PARTS = 3
+TILE = 256
+STEP = 128
+
+def dot_nt(a,b): return lax.dot_general(a,b,(((1,),(1,)),((),())),preferred_element_type=f32)
+def dot_nn(a,b): return jnp.dot(a,b,preferred_element_type=f32)
+
+def lane_row(test, wide, kind=f32):
+    lane = lax.broadcasted_iota(jnp.int32, (1, wide), 1)
+    return jnp.where(test(lane), 1.0, 0.0).astype(kind)
+
+def part_rows(wide, start):
+    return [lane_row(lambda l: l == start + n, wide) for n in range(PARTS)]
+
+def spread(column, rows):
+    top = column.astype(bf16).astype(f32)
+    return (top*rows[0] + (column-top)*rows[1]).astype(bf16)
+
+def cross_ones(wide, hd):
+    a = lax.broadcasted_iota(jnp.int32, (wide, wide), 0) < hd
+    b = lax.broadcasted_iota(jnp.int32, (wide, wide), 1) < hd
+    return jnp.where(a != b, 1.0, 0.0).astype(bf16)
+
+def side_rows(wide, hd):
+    return [lane_row(lambda l: l < hd, wide, bf16), lane_row(lambda l: l >= hd, wide, bf16)]
+
+def marks(plan, span, wide, hd, side):
+    place = lax.broadcasted_iota(jnp.int32, (span, wide), 0)
+    lane = lax.broadcasted_iota(jnp.int32, (span, wide), 1) - (hd if side == 0 else 0)
+    lane = jnp.where((lane >= 0) & (lane < hd), lane, hd)
+    seg = jnp.zeros((span, wide), jnp.int32)
+    for n in range(SEGS-1):
+        seg = seg + jnp.where(place >= plan[1+n], 1, 0)
+    hit = lane == seg
+    asked = jnp.where((lane < SEGS) & (lane != seg), 1.0, 0.0).astype(bf16)
+    held = jnp.where(hit, -1e30, jnp.where((lane >= SEGS) & (lane < SEGS+PARTS), 1.0, 0.0)).astype(bf16)
+    return asked, held
+
+def by_half(mine, work):
+    for n in range(2):
+        @pl.when(mine == n)
+        def _():
+            work(n)
+
+def query_tiles(plan, span, work, broad=512):
+    tiles = span//TILE
+    fewest = plan[5+tiles]
+    for n in range(1, tiles):
+        fewest = jnp.minimum(fewest, plan[5+tiles+n])
+    @pl.when(fewest == tiles)
+    def _():
+        def one(i, carry):
+            work(pl.ds(pl.multiple_of(i*broad, broad), broad), slice(0, span))
+            return carry
+        lax.fori_loop(0, span//broad, one, 0)
+    @pl.when(fewest < tiles)
+    def _():
+        def one(i, carry):
+            rows = pl.ds(pl.multiple_of(i*TILE, TILE), TILE)
+            start = pl.multiple_of(plan[5+i]*STEP, STEP)
+            for n in range(1, tiles+1):
+                @pl.when(plan[5+tiles+i] == n)
+                def _():
+                    work(rows, pl.ds(start, n*TILE) if n < tiles else slice(0, span))
+            return carry
+        lax.fori_loop(0, tiles, one, 0)
+
+def attend_kernel(plan, xo_ref, xp_ref, own_ref, par_ref, qa_ref, qf, kf, ka, va, og, outs, *, hd):
+    half = xo_ref.shape[0]
+    span = 2*half
+    wide = 2*hd
+    sides = side_rows(wide, hd)
+    swap = cross_ones(wide, hd)
+    first = lax.broadcasted_iota(jnp.int32, (span, wide), 1) < hd
+    start = [hd+SEGS, SEGS]
+    parts = [part_rows(wide, start[s]) for s in range(2)]
+    @pl.when(pl.program_id(0) == 0)
+    def _():
+        for s in range(2):
+            qf[s], kf[s] = marks(plan, span, wide, hd, s)
+    longest = None
+    for x_ref in (xo_ref, xp_ref):
+        kp = x_ref[:, wide:2*wide]
+        norms = jnp.max(dot_nn(kp*kp, swap), axis=0, keepdims=True)
+        longest = norms if longest is None else jnp.maximum(longest, norms)
+    def place(n):
+        for x_ref, at in ((xo_ref, n), (xp_ref, 1-n)):
+            rows = slice(at*half, (at+1)*half)
+            qp = x_ref[:, 0:wide]
+            kp = x_ref[:, wide:2*wide]
+            vp = x_ref[:, 2*wide:3*wide]
+            top = jnp.sqrt(dot_nn(qp*qp, swap) * longest) * 1.02
+            for s in range(2):
+                qa_ref[s, rows, :] = qp*sides[s] + (qf[s, rows, :] - (top*parts[s][0]).astype(bf16))
+                ka[s, rows, :] = kp*sides[s] + kf[s, rows, :]
+                va[s, rows, :] = vp*sides[s] + sides[1-s]
+    by_half(plan[0], place)
+    def weigh(rows, keys):
+        for s in range(2):
+            w = jnp.exp2(dot_nt(qa_ref[s, rows, :], ka[s, keys, :])).astype(bf16)
+            og[s, rows, :] = dot_nn(w, va[s, keys, :])
+    query_tiles(plan, span, weigh)
+    @pl.when(jnp.logical_not(jnp.min(jnp.where(first, og[1], og[0])) > 2.0**-80))
+    def _():
+        def exact_tile(i, carry):
+            rows = pl.ds(pl.multiple_of(i*TILE, TILE), TILE)
+            for s in range(2):
+                plain = qa_ref[s, rows, :] * (1.0 - parts[s][0]).astype(bf16)
+                m = jnp.max(dot_nt(plain, ka[s]), axis=1, keepdims=True)
+                qa_ref[s, rows, :] = plain - (jnp.broadcast_to(m, (TILE, wide))*parts[s][0]).astype(bf16)
+            weigh(rows, slice(0, span))
+            return carry
+        lax.fori_loop(0, span//TILE, exact_tile, 0)
+    total = jnp.where(first, og[1], og[0])
+    outs[...] = (jnp.where(first, og[0], og[1]) / pltpu.roll(total, hd, 1)).astype(bf16)
+    lse = -jnp.log2(total)
+    for s in range(2):
+        qa_ref[s] = qa_ref[s] + spread(lse, parts[s][1:])
+    def leave(n):
+        own_ref[...] = outs[n*half:(n+1)*half, :]
+        par_ref[...] = outs[(1-n)*half:(2-n)*half, :]
+    by_half(plan[0], leave)
+
+def attend(plan, qkv_own, qkv_par, heads, hd):
+    half = qkv_own.shape[0]; span = 2*half; mine = heads*hd; wide = 2*hd
+    col = lambda p, s: (0, p)
+    return pl.pallas_call(
+        functools.partial(attend_kernel, hd=hd),
+        grid_spec=pltpu.PrefetchScalarGridSpec(
+            num_scalar_prefetch=1, grid=(heads//2,),
+            in_specs=[pl.BlockSpec((half, 3*wide), col)]*2,
+            out_specs=[
+                pl.BlockSpec((half, wide), col),
+                pl.BlockSpec((half, wide), col),
+                pl.BlockSpec((2, span, wide), lambda p, s: (p, 0, 0)),
+            ],
+            scratch_shapes=[
+                pltpu.VMEM((2, span, wide), bf16),
+                pltpu.VMEM((2, span, wide), bf16),
+                pltpu.VMEM((2, span, wide), bf16),
+                pltpu.VMEM((2, span, wide), bf16),
+                pltpu.VMEM((2, span, wide), f32),
+                pltpu.VMEM((span, wide), bf16),
+            ]),
+        out_shape=[
+            jax.ShapeDtypeStruct((half, mine), bf16),
+            jax.ShapeDtypeStruct((half, mine), bf16),
+            jax.ShapeDtypeStruct((heads, span, wide), bf16),
+        ],
+        compiler_params=pltpu.CompilerParams(vmem_limit_bytes=32<<20),
+        cost_estimate=pl.CostEstimate(flops=4*span*span*mine, bytes_accessed=span*mine*12, transcendentals=span*span*heads),
+    )(plan, qkv_own, qkv_par)
+
+def attend_back_kernel(plan, xo_ref, xp_ref, co_ref, cp_ref, go_ref, gp_ref, qa_ref, own_ref, par_ref, kf, ka, va, ga, kt, kacc, vacc, qacc, *, hd):
+    half = xo_ref.shape[0]
+    span = 2*half
+    wide = 2*hd
+    sides = side_rows(wide, hd)
+    low = [lane_row(lambda l: (l >= hd) & (l < hd+PARTS), wide, bf16), lane_row(lambda l: l < PARTS, wide, bf16)]
+    parts = [part_rows(wide, hd), part_rows(wide, 0)]
+    swap = cross_ones(wide, hd)
+    first = lax.broadcasted_iota(jnp.int32, (half, wide), 1) < hd
+    @pl.when(pl.program_id(0) == 0)
+    def _():
+        for s in range(2):
+            kf[s] = marks(plan, span, wide, hd, s)[1]
+    def place(n):
+        for x_ref, c_ref, g_ref, at in ((xo_ref, co_ref, go_ref, n), (xp_ref, cp_ref, gp_ref, 1-n)):
+            rows = slice(at*half, (at+1)*half)
+            kp = x_ref[:, wide:2*wide]
+            vp = x_ref[:, 2*wide:3*wide]
+            gp = g_ref[...]
+            kt[:, rows] = kp.T
+            prod = gp.astype(f32) * c_ref[...].astype(f32)
+            top = prod.astype(bf16)
+            delta = dot_nn(top, swap) + dot_nn((prod - top.astype(f32)).astype(bf16), swap)
+            for s in range(2):
+                ka[s, rows, :] = kp*sides[s] + kf[s, rows, :]
+                va[s, rows, :] = vp*sides[s] + low[s]
+                ga[s, rows, :] = gp*sides[s] + spread(-delta, parts[s])
+    by_half(plan[0], place)
+    kacc[...] = jnp.zeros_like(kacc)
+    vacc[...] = jnp.zeros_like(vacc)
+    def work(rows, keys):
+        for s in range(2):
+            qq = qa_ref[s, rows, :]
+            gg = ga[s, rows, :]
+            probs = jnp.exp2(dot_nt(ka[s, keys, :], qq))
+            slope = (probs * dot_nt(va[s, keys, :], gg)).astype(bf16)
+            vacc[s, keys, :] += dot_nn(probs.astype(bf16), gg)
+            kacc[s, keys, :] += dot_nn(slope, qq)
+            qacc[s*hd:(s+1)*hd, rows] = dot_nn(kt[s*hd:(s+1)*hd, keys], slope)
+    query_tiles(plan, span, work, TILE)
+    def leave(n):
+        for o_ref, at in ((own_ref, n), (par_ref, 1-n)):
+            rows = slice(at*half, (at+1)*half)
+            o_ref[:, 0:wide] = (qacc[:, rows].T * LN2).astype(bf16)
+            o_ref[:, wide:2*wide] = (jnp.where(first, kacc[0, rows, :], kacc[1, rows, :]) * LN2).astype(bf16)
+            o_ref[:, 2*wide:3*wide] = jnp.where(first, vacc[0, rows, :], vacc[1, rows, :]).astype(bf16)
+    by_half(plan[0], leave)
+
+def attend_back(plan, qkv_own, qkv_par, ctx_own, ctx_par, g_own, g_par, qa, heads, hd):
+    half = qkv_own.shape[0]; span = 2*half; mine = heads*hd; wide = 2*hd
+    col = lambda p, s: (0, p)
+    return pl.pallas_call(
+        functools.partial(attend_back_kernel, hd=hd),
+        grid_spec=pltpu.PrefetchScalarGridSpec(
+            num_scalar_prefetch=1, grid=(heads//2,),
+            in_specs=[pl.BlockSpec((half, 3*wide), col)]*2 + [pl.BlockSpec((half, wide), col)]*4 + [pl.BlockSpec((2, span, wide), lambda p, s: (p, 0, 0))],
+            out_specs=[pl.BlockSpec((half, 3*wide), col)]*2,
+            scratch_shapes=[
+                pltpu.VMEM((2, span, wide), bf16),
+                pltpu.VMEM((2, span, wide), bf16),
+                pltpu.VMEM((2, span, wide), bf16),
+                pltpu.VMEM((2, span, wide), bf16),
+                pltpu.VMEM((wide, span), bf16),
+                pltpu.VMEM((2, span, wide), f32),
+                pltpu.VMEM((2, span, wide), f32),
+                pltpu.VMEM((wide, span), f32),
+            ]),
+        out_shape=[jax.ShapeDtypeStruct((half, 3*mine), bf16)]*2,
+        compiler_params=pltpu.CompilerParams(vmem_limit_bytes=40<<20),
+        cost_estimate=pl.CostEstimate(flops=10*span*span*mine, bytes_accessed=span*mine*20, transcendentals=span*span*heads),
+    )(plan, qkv_own, qkv_par, ctx_own, ctx_par, g_own, g_par, qa)
+
+def plan_row(lengths, my_block, span):
+    bounds = jnp.cumsum(lengths)
+    place = jnp.arange(span, dtype=jnp.int32)
+    edges = jnp.concatenate([jnp.zeros((1,), jnp.int32), bounds, jnp.full((1,), span, jnp.int32)]).astype(jnp.int32)
+    seg = jnp.sum((place[:, None] >= bounds[None, :]).astype(jnp.int32), axis=1)
+    lo = edges[seg[0::TILE]]
+    hi = edges[seg[TILE-1::TILE]+1]
+    begin = lo // STEP
+    count = (hi - begin*STEP + TILE-1)//TILE
+    begin = jnp.minimum(begin, (span - count*TILE)//STEP)
+    return jnp.concatenate([jnp.reshape(my_block, (1,)).astype(jnp.int32), bounds.astype(jnp.int32), begin.astype(jnp.int32), count.astype(jnp.int32)])
+
+
+def centred(hidden):
+    off = hidden - jnp.mean(hidden, axis=-1, keepdims=True)
+    scale = lax.rsqrt(jnp.mean(off*off, axis=-1, keepdims=True) + 1e-05)
+    return off*scale, scale
+
+def norm_back(grad, unit, scale):
+    inner = jnp.mean(grad*unit, axis=-1, keepdims=True)
+    return scale*(grad - jnp.mean(grad, axis=-1, keepdims=True) - unit*inner)
+
+def gelu_pair(x):
+    size = jnp.abs(x)
+    base = 1.0 + size*(0.3275911*0.7071067811865476)
+    t = pl.reciprocal(base, approx=True)
+    t = t*(2.0 - base*t)
+    bell = jnp.exp2(x*x*(-0.7213475204444817))
+    tail = t*(0.127414796 + t*(-0.142248368 + t*(0.7107068705 + t*(-0.7265760135 + t*0.5307027145))))*bell
+    below = jnp.where(x < 0, tail, 1.0 - tail)
+    return x*below, below + x*(bell*0.3989422804014327)
+
+def ffn_kernel(place, co_ref, cr_ref, x_ref, cot_ref, g1_ref, g2_ref, pack_ref, out_ref, grad_ref, own_ref, send_ref, wo, wi, wb, slopes, gsum, sems, *, shards, cuts):
+    width = x_ref.shape[1]
+    lead = wo.shape[1]
+    back = wb.shape[1]
+    copies = [pltpu.make_async_copy(pack_ref.at[:, 0:lead, :], wo, sems.at[0])]
+    for j in range(cuts):
+        copies.append(pltpu.make_async_copy(pack_ref.at[:, lead*(1+j):lead*(2+j), :], wi.at[j], sems.at[1+j]))
+    per = shards//cuts
+    for j in range(cuts):
+        copies.append(pltpu.make_async_copy(pack_ref.at[j*per:(j+1)*per, lead*(1+cuts):lead*(1+cuts)+back, :], wb.at[j*per:(j+1)*per], sems.at[1+cuts+j]))
+    for c in copies:
+        c.start()
+    part = shards//2
+    half = width//2
+    mine = place[0]
+    def out_rows(who):
+        return wo[pl.ds(pl.multiple_of(who*part, part), part)].reshape(half, width)
+    def w_in(j): return wi[j].reshape(width, width)
+    def w_back(j): return wb[j*per:(j+1)*per].reshape(per*back, width)
+    copies[0].wait()
+    resid = x_ref[...].astype(f32) + dot_nn(co_ref[...], out_rows(mine)) + dot_nn(cr_ref[...], out_rows(1-mine))
+    unit_one, scale_one = centred(resid)
+    normed = unit_one*g1_ref[...]
+    low = normed.astype(bf16)
+    total = normed
+    for j in range(cuts):
+        copies[1+j].wait()
+        pre = dot_nn(low, w_in(j))
+        act, slope = gelu_pair(pre)
+        slopes[j] = slope.astype(bf16)
+        copies[1+cuts+j].wait()
+        total = total + dot_nn(act.astype(bf16), w_back(j))
+    unit_two, scale_two = centred(total)
+    out_ref[...] = (unit_two*g2_ref[...]).astype(bf16)
+    grad_two = norm_back(cot_ref[...].astype(f32)*g2_ref[...], unit_two, scale_two)
+    low_two = grad_two.astype(bf16)
+    grad = grad_two
+    for j in range(cuts):
+        pre_grad = (dot_nt(low_two, w_back(j))*slopes[j].astype(f32)).astype(bf16)
+        grad = grad + dot_nt(pre_grad, w_in(j))
+    grad_one = norm_back(grad*g1_ref[...], unit_one, scale_one)
+    grad_ref[...] = grad_one
+    low_one = grad_one.astype(bf16)
+    own_ref[...] = dot_nt(low_one, out_rows(mine)).astype(bf16)
+    send_ref[...] = dot_nt(low_one, out_rows(1-mine)).astype(bf16)
+
+def ffn(place, ctx_own, ctx_recv, x, cot, gain_one, gain_two, pack, cuts):
+    span, width = x.shape
+    shards, total, _ = pack.shape
+    lead = width//shards
+    back = cuts*width//shards
+    whole = lambda shape: pl.BlockSpec(shape, lambda i, s: (0,)*len(shape))
+    return pl.pallas_call(
+        functools.partial(ffn_kernel, shards=shards, cuts=cuts),
+        grid_spec=pltpu.PrefetchScalarGridSpec(
+            num_scalar_prefetch=1, grid=(1,),
+            in_specs=[whole((span, width//2)), whole((span, width//2)), whole((span, width)), whole((span, width)), whole((1, width)), whole((1, width)), pl.BlockSpec(memory_space=pl.ANY)],
+            out_specs=[whole((span, width)), whole((span, width)), whole((span, width//2)), whole((span, width//2))],
+            scratch_shapes=[
+                pltpu.VMEM((shards, lead, width), bf16),
+                pltpu.VMEM((cuts, shards, lead, width), bf16),
+                pltpu.VMEM((shards, back, width), bf16),
+                pltpu.VMEM((cuts, span, width), bf16),
+                pltpu.VMEM((8, 128), f32),
+                pltpu.SemaphoreType.DMA((1+2*cuts,)),
+            ]),
+        out_shape=[
+            jax.ShapeDtypeStruct((span, width), bf16),
+            jax.ShapeDtypeStruct((span, width), f32),
+            jax.ShapeDtypeStruct((span, width//2), bf16),
+            jax.ShapeDtypeStruct((span, width//2), bf16),
+        ],
+        compiler_params=pltpu.CompilerParams(vmem_limit_bytes=56<<20),
+        cost_estimate=pl.CostEstimate(flops=2*span*width*width*(2+4*cuts), bytes_accessed=2*(2+2*cuts)*width*width, transcendentals=2*span*width*cuts),
+    )(place, ctx_own, ctx_recv, x, cot, gain_one, gain_two, pack)
 
 
 def shifted(shard, axis, by):
@@ -61,7 +405,7 @@
     return (query_grad, key_grad, value_grad)
 
 
-def body(
+def body_any(
     tokens,
     sent_lengths,
     w_query,
@@ -229,9 +573,149 @@
     )
 
 
+def swapped(block):
+    return lax.ppermute(block, "blk", [(0, 1), (1, 0)])
+
+
+def summed(vector, groups):
+    vector = vector + swapped(vector)
+    hop = 1
+    while hop < groups:
+        vector = vector + lax.ppermute(vector, "seq", [(i, i ^ hop) for i in range(groups)])
+        hop *= 2
+    return vector
+
+
+def body_two(
+    tokens,
+    sent_lengths,
+    w_query,
+    w_key,
+    w_value,
+    w_out,
+    shared_a,
+    shared_b,
+    w_in,
+    w_back,
+    gain_one,
+    gain_two,
+    scale_dq,
+    shift_bq,
+    scale_dv,
+    shift_bv,
+    cotangent,
+):
+    row_count, span, width = tokens.shape
+    shards = lax.axis_size("seq")
+    mine = lax.axis_index("blk")
+    heads = HEADS // 2
+    part = heads * HEAD_DIM
+    wide = 2 * HEAD_DIM
+    pairs = heads // 2
+    rank = shared_a.shape[1]
+    cuts = w_in.shape[1] // width
+    coef = 0.125 * LOG2E
+
+    def columns(matrix):
+        return lax.dynamic_slice_in_dim(matrix, mine * part, part, matrix.ndim - 1)
+
+    def paired(triple):
+        return [piece[..., n * wide : (n + 1) * wide] for n in range(pairs) for piece in triple]
+
+    up = columns(shared_b)
+    lead = shared_a.shape[0]
+    first_pack = jnp.concatenate(
+        [shared_a]
+        + paired([columns(w_query), columns(w_key), columns(w_value)])
+        + [up.reshape(lead, up.size // lead)],
+        axis=1,
+    )
+    other = [swapped(tokens[row]) for row in range(row_count)]
+    gathered = lax.all_gather(first_pack, "seq", axis=0)
+    second_pack = jnp.concatenate(
+        [w_out] + [w_in[:, n * width : (n + 1) * width] for n in range(cuts)] + [w_back], axis=0
+    )
+    pack = lax.all_gather(second_pack, "seq", axis=0)
+    down = gathered[:, :, :rank].reshape(width, rank)
+    mixed = gathered[:, :, rank : rank + 3 * part].reshape(width, 3 * part)
+    lift = gathered[:, :, rank + 3 * part :].reshape(rank, part)
+    lift_f = lift.astype(f32)
+    inner = jnp.concatenate([lift_f * scale_dq[:, None], lift_f * scale_dv[:, None]], axis=1)
+    merged = dot_nn(down, inner.astype(bf16))
+    bend_q = columns(shift_bq)
+    bend_v = columns(shift_bv)
+    mixed_f = mixed.astype(f32)
+    blocks = []
+    for n in range(pairs):
+        at = slice(n * wide, (n + 1) * wide)
+        base = 3 * n * wide
+        delta_q = merged[:, at] * bend_q[at]
+        delta_v = merged[:, part + n * wide : part + (n + 1) * wide] * bend_v[at]
+        blocks.append((mixed_f[:, base : base + wide] + delta_q) * coef)
+        blocks.append(mixed_f[:, base + wide : base + 2 * wide])
+        blocks.append(mixed_f[:, base + 2 * wide : base + 3 * wide] + delta_v)
+    weights = jnp.concatenate(blocks, axis=1).astype(bf16)
+    place = jnp.reshape(mine, (1,)).astype(jnp.int32)
+    g_one = gain_one.reshape(1, width)
+    g_two = gain_two.reshape(1, width)
+
+    rows = range(row_count)
+    plans = [plan_row(sent_lengths[row], mine, 2 * span) for row in rows]
+    qkv_own = [dot_nn(tokens[row], weights).astype(bf16) for row in rows]
+    qkv_par = [dot_nn(other[row], weights).astype(bf16) for row in rows]
+    seen = [attend(plans[row], qkv_own[row], qkv_par[row], heads, HEAD_DIM) for row in rows]
+    ctx_recv = [swapped(seen[row][1]) for row in rows]
+    fed = [
+        ffn(place, seen[row][0], ctx_recv[row], tokens[row], cotangent[row], g_one, g_two, pack, cuts)
+        for row in rows
+    ]
+    grad_recv = [swapped(fed[row][3]) for row in rows]
+    turned = [
+        attend_back(
+            plans[row], qkv_own[row], qkv_par[row], seen[row][0], seen[row][1],
+            fed[row][2], grad_recv[row], seen[row][2], heads, HEAD_DIM,
+        )
+        for row in rows
+    ]
+    sent = [swapped(dot_nt(turned[row][1], weights).astype(bf16)) for row in rows]
+    token_grad = [
+        (fed[row][1] + dot_nt(turned[row][0], weights) + sent[row].astype(f32)).astype(bf16)
+        for row in rows
+    ]
+
+    def outer(left, right):
+        return lax.dot_general(left, right, (((0,), (0,)), ((), ())), preferred_element_type=f32)
+
+    moment = sum(outer(tokens[row], turned[row][0]) + outer(other[row], turned[row][1]) for row in rows)
+    moment_q = jnp.concatenate([moment[:, 3 * n * wide : (3 * n + 1) * wide] for n in range(pairs)], axis=1)
+    moment_v = jnp.concatenate(
+        [moment[:, (3 * n + 2) * wide : (3 * n + 3) * wide] for n in range(pairs)], axis=1
+    )
+    moment_q = moment_q * coef
+    down_f = down.astype(f32)
+
+    def whole(piece):
+        return lax.dynamic_update_slice(jnp.zeros((width,), f32), piece, (mine * part,))
+
+    part_bq = whole(jnp.sum(merged[:, :part] * moment_q, axis=0))
+    part_bv = whole(jnp.sum(merged[:, part:] * moment_v, axis=0))
+    part_dq = jnp.sum(down_f * dot_nt((moment_q * bend_q).astype(bf16), lift), axis=0)
+    part_dv = jnp.sum(down_f * dot_nt((moment_v * bend_v).astype(bf16), lift), axis=0)
+    flat = jnp.concatenate([part_dq, part_bq, part_dv, part_bv]).reshape(-1, 128)
+    flat = summed(flat, shards).reshape(-1)
+    return (
+        jnp.stack([fed[row][0] for row in rows]),
+        jnp.stack(token_grad),
+        flat[:rank],
+        flat[rank : rank + width],
+        flat[rank + width : 2 * rank + width],
+        flat[2 * rank + width :],
+    )
+
+
 def solution(mesh):
     return jax.shard_map(
-        body,
+        body_two if mesh.shape["blk"] == 2 else body_any,
         mesh=mesh,
         in_specs=(
             P("seq", "blk", None),

time: 952 us -> 331 us (0.35)
  waiting for transfers between devices: 484 us -> 77.2 us
  matrix products: 278 us -> 24.1 us
  Pallas kernels: 0 us -> 144 us
  other arithmetic: 52.9 us -> 9.61 us
  blocking collectives: 39.6 us -> 0 us
  local copies, waits for them, and re-layouts: 67.2 us -> 37.9 us
    dot_general x29 -> x15, matrix products: 278 us -> 24.1 us  [the longest x5 9.28 us: dot_nn(): return jnp.dot(a, b, preferred_element_type=f32)]
    all_gather x10 -> x2, waiting for transfers between devices: 270 us -> 47 us  [the longest x1 36.7 us: body_two(): gathered = lax.all_gather(first_pack, 'seq', axis=0)]
    ppermute x8 -> x13, waiting for transfers between devices: 209 us -> 30.2 us  [the longest x9 28.7 us: swapped(): return lax.ppermute(block, 'blk', [(0, 1), (1, 0)])]
    pallas_call x0 -> x6, Pallas kernels: none -> 144 us  [the longest x2 54.6 us: attend(): pl.pallas_call(functools.partial(attend_kernel, hd=hd), grid_spec=pltpu.P...]
    psum x1 -> x0, blocking collectives: 39.6 us -> none  [body(): lax.psum((part_dq, part_bq, part_dv, part_bv), ('seq', 'blk'))]
    reduce_sum x7 -> x3, other arithmetic: 30.3 us -> 1.14 us  [the longest x1 0.97 us: body_two(): part_bq = whole(jnp.sum(merged[:, :part] * moment_q, axis=0))]
    convert_element_type x7 -> x1, other arithmetic: 18.6 us -> 0.37 us  [body_two(): mixed_f = mixed.astype(f32)]
    convert_element_type x10 -> x0, local copies, waits for them, and re-layouts: 16.4 us -> none  [the longest x2 4.21 us: body(): value_grad = value_acc.reshape(token_count, width).astype(jnp.bfloat16)]
  transfers between devices with their start and end apart: 18 -> 15, of which waited for: 17 -> 6; matrix products, arithmetic and copies ran while one was open for 24% -> 14% of each run, Pallas kernels for 0% -> 37%
where the time goes in v1:
time: 331 us; the launch traced here: 326 us
  Pallas kernels  144 us (44%)
  waiting for transfers between devices  77.2 us (23%)
  local copies, waits for them, and re-layouts  37.9 us (11%)
  matrix products  24.1 us (7%)
  starting transfers between devices  17.9 us (5%)
  between operations  15.1 us (5%)
  other arithmetic  9.61 us (3%)
    pallas_call x2, Pallas kernels, attend(): pl.pallas_call(functools.partial(attend_kernel, hd=hd), grid_spec=pltpu.P...  54.6 us
    pallas_call x2, Pallas kernels, ffn(): pl.pallas_call(functools.partial(ffn_kernel, shards=shards, cuts=cuts), g...  49.2 us
    pallas_call x2, Pallas kernels, attend_back(): pl.pallas_call(functools.partial(attend_back_kernel, hd=hd), grid_spec=pl...  40.5 us
    all_gather x1, waiting for transfers between devices, body_two(): gathered = lax.all_gather(first_pack, 'seq', axis=0)  36.7 us
    ppermute x9, waiting for transfers between devices, swapped(): return lax.ppermute(block, 'blk', [(0, 1), (1, 0)])  28.7 us
    unnamed x118, local copies, waits for them, and re-layouts  21.6 us
    ppermute x9, starting transfers between devices, swapped(): return lax.ppermute(block, 'blk', [(0, 1), (1, 0)])  10.4 us
    all_gather x1, waiting for transfers between devices, body_two(): pack = lax.all_gather(second_pack, 'seq', axis=0)  10.3 us
  transfers between devices with their start and end apart: 15, of which 6 were waited for; matrix products, arithmetic and copies ran while one was open for 14% of the time, Pallas kernels for 37%

profile of v1, /device:TPU:0, one launch (start us, length us, event | category | flops | bytes accessed | tf_op | source)
XLA Modules:
  0.0 326.1 jit_solution(8944139751138181497)
XLA Ops:
  23.0 2.9 collective-permute-start
  32.9 36.7 %all-gather.5.cloned.1.call-done = bf16[768,2688]{1,0:T(8,128)(2,1)} async-done(((bf16[48,2688]{1,0:T(8,128)(2,1)}), bf16[768,2688]{1,0:T(8,128)(2,1)}) %all-gather.5.cloned.1.call-update) | async-done | bytes 4128784 | tf_op jit(solution)/shard_map/all_gather | solution.py:634
  70.8 2.7 slice.271
  73.5 1.6 slice.269
  76.6 1.6 fusion.8
  83.2 2.8 fusion.7.xp_ref
  86.0 26.9 %shard_map.210 = (bf16[512,384]{1,0:T(8,128)(2,1)S(1)}, bf16[512,384]{1,0:T(8,128)(2,1)S(1)}, bf16[6,1024,128]{2,1,0:T(8,128)(2,1)S(1)}) custom-call(s32[13]{0:T(128)S(1)} %pad_add_fusion.5.plan, bf16[512,1152]{1,0:T(8,128)(2,1)S(1)} %fusion.6.xo_ref, bf16[512,1152]{1,0:T(8,128)(2,1)S(1)} %fusion.7.xp_ref), custom_call_target="tpu_custom_call" | custom-call | flops 1610612736 | bytes 4718592 | tf_op jit(solution)/shard_map/pallas_call | solution.py:146
  113.0 1.5 collective-permute-start.3
  115.7 2.8 fusion.5.xp_ref
  118.5 27.7 %shard_map.208 = (bf16[512,384]{1,0:T(8,128)(2,1)S(1)}, bf16[512,384]{1,0:T(8,128)(2,1)S(1)}, bf16[6,1024,128]{2,1,0:T(8,128)(2,1)S(1)}) custom-call(s32[13]{0:T(128)S(1)} %pad_add_fusion.4.plan, bf16[512,1152]{1,0:T(8,128)(2,1)S(1)} %fusion.4.xo_ref, bf16[512,1152]{1,0:T(8,128)(2,1)S(1)} %fusion.5.xp_ref), custom_call_target="tpu_custom_call" | custom-call | flops 1610612736 | bytes 4718592 | tf_op jit(solution)/shard_map/pallas_call | solution.py:146
  148.8 10.3 %all-gather.7.cloned.1.call-done = bf16[6912,768]{1,0:T(8,128)(2,1)} async-done(((bf16[432,768]{1,0:T(8,128)(2,1)}), bf16[6912,768]{1,0:T(8,128)(2,1)}) %all-gather.7.cloned.1.call-update) | async-done | bytes 10616848 | tf_op jit(solution)/shard_map/all_gather | solution.py:638
  159.1 24.3 %shard_map.211 = (bf16[512,768]{1,0:T(8,128)(2,1)}, f32[512,768]{1,0:T(8,128)}, bf16[512,384]{1,0:T(8,128)(2,1)}, bf16[512,384]{1,0:T(8,128)(2,1)}) custom-call(s32[1]{0:T(128)} %bitcast.place, bf16[512,384]{1,0:T(8,128)(2,1)} %copy-done.20, bf16[512,384]{1,0:T(8,128)(2,1)} %copy-done.49, bf16[512,768]{1,0:T(8,128)(2,1)} %get-tuple-element.59.x_ref, ...), custom_call_target="tpu_custom_call" | custom-call | flops 10871635968 | bytes 11796480 | tf_op jit(solution)/shard_map/pallas_call | solution.py:329
  183.4 1.5 collective-permute-start.6
  185.7 24.9 %shard_map.209 = (bf16[512,768]{1,0:T(8,128)(2,1)}, f32[512,768]{1,0:T(8,128)}, bf16[512,384]{1,0:T(8,128)(2,1)}, bf16[512,384]{1,0:T(8,128)(2,1)}) custom-call(s32[1]{0:T(128)} %bitcast.place, bf16[512,384]{1,0:T(8,128)(2,1)} %copy-done.18, bf16[512,384]{1,0:T(8,128)(2,1)} %copy-done.48, bf16[512,768]{1,0:T(8,128)(2,1)} %get-tuple-element.58.x_ref, ...), custom_call_target="tpu_custom_call" | custom-call | flops 10871635968 | bytes 11796480 | tf_op jit(solution)/shard_map/pallas_call | solution.py:329
  211.3 17.4 %shard_map.213 = (bf16[512,1152]{1,0:T(8,128)(2,1)S(1)}, bf16[512,1152]{1,0:T(8,128)(2,1)S(1)}) custom-call(s32[13]{0:T(128)S(1)} %pad_add_fusion.5.plan, bf16[512,1152]{1,0:T(8,128)(2,1)S(1)} %copy-done.11, bf16[512,1152]{1,0:T(8,128)(2,1)S(1)} %copy-done.13, bf16[512,384]{1,0:T(8,128)(2,1)S(1)} %copy-done.21, ...), custom_call_target="tpu_custom_call" | custom-call | flops 4026531840 | bytes 7864320 | tf_op jit(solution)/shard_map/pallas_call | solution.py:224
  228.7 2.5 fusion.53
  233.7 23.1 %shard_map.212 = (bf16[512,1152]{1,0:T(8,128)(2,1)S(1)}, bf16[512,1152]{1,0:T(8,128)(2,1)S(1)}) custom-call(s32[13]{0:T(128)S(1)} %pad_add_fusion.4.plan, bf16[512,1152]{1,0:T(8,128)(2,1)S(1)} %copy-done.7, bf16[512,1152]{1,0:T(8,128)(2,1)S(1)} %copy-done.9, bf16[512,384]{1,0:T(8,128)(2,1)S(1)} %copy-done.19, bf16[512,384]{1,0:T(8,128)(2,1)S(1)} %copy-done.5, ...), custom_call_target="tpu_custom_call" | custom-call | flops 4026531840 | bytes 7864320 | tf_op jit(solution)/shard_map/pallas_call | solution.py:224
  256.8 2.8 fusion.52
  267.4 1.5 collective-permute-start.8
  269.0 2.8 pad_maximum_fusion
  273.1 2.5 collective-permute-start.10
  277.4 3.4 %collective-permute-start.11 = (f32[28,128]{1,0:T(8,128)S(1)}, f32[28,128]{1,0:T(8,128)S(1)}, u32[]{:S(2)}, u32[]{:S(2)}) collective-permute-start(f32[28,128]{1,0:T(8,128)S(1)} %add.128), channel_id=1, source_target_pairs={{0,8},{2,10},{4,12},{6,14},{8,0},{10,2},{12,4},{14,6},{16,24},{18,... | collective-permute-start | bytes 43016 | tf_op jit(solution)/shard_map/ppermute | solution.py:584
  288.6 14.0 %collective-permute-done.7 = bf16[512,768]{1,0:T(8,128)(2,1)S(1)} collective-permute-done((bf16[512,768]{1,0:T(8,128)(2,1)S(1)}, bf16[512,768]{1,0:T(8,128)(2,1)S(1)}, u32[]{:S(2)}, u32[]{:S(2)}) %collective-permute-start.7) | collective-permute-done | bytes 786464 | tf_op jit(solution)/shard_map/ppermute | solution.py:577
  302.8 14.6 %collective-permute-done.5 = bf16[512,768]{1,0:T(8,128)(2,1)S(1)} collective-permute-done((bf16[512,768]{1,0:T(8,128)(2,1)S(1)}, bf16[512,768]{1,0:T(8,128)(2,1)S(1)}, u32[]{:S(2)}, u32[]{:S(2)}) %collective-permute-start.5) | collective-permute-done | bytes 786464 | tf_op jit(solution)/shard_map/ppermute | solution.py:577
  (213 shorter events, 58.1 us)
Async XLA Ops:
  7.2 62.4 %all-gather.5.cloned.1.call-start = ((), (), s32[]{:S(2)}) async-start(), calls=%async_computation | async-start | bytes 4386816 | tf_op jit(solution)/shard_map/all_gather | solution.py:634
  16.2 142.9 %all-gather.7.cloned.1.call-start = ((), (), s32[]{:S(2)}) async-start(), calls=%async_computation.1 | async-start | bytes 11280384 | tf_op jit(solution)/shard_map/all_gather | solution.py:638
  23.0 92.8 %collective-permute-start = (bf16[512,768]{1,0:T(8,128)(2,1)}, bf16[512,768]{1,0:T(8,128)(2,1)}, u32[]{:S(2)}, u32[]{:S(2)}) collective-permute-start(bf16[512,768]{1,0:T(8,128)(2,1)} %get-tuple-element.58.x_ref), channel_id=1, source_target_pairs={{0,1},{1,0},{2,3},{3,2},{4,5},{5,4},{6,7},{7,6},{8,9},{9,8},{10,11... | collective-permute-start | bytes 2359304 | tf_op jit(solution)/shard_map/ppermute | solution.py:577
  25.9 57.4 %collective-permute-start.2 = (bf16[512,768]{1,0:T(8,128)(2,1)}, bf16[512,768]{1,0:T(8,128)(2,1)}, u32[]{:S(2)}, u32[]{:S(2)}) collective-permute-start(bf16[512,768]{1,0:T(8,128)(2,1)} %get-tuple-element.59.x_ref), channel_id=1, source_target_pairs={{0,1},{1,0},{2,3},{3,2},{4,5},{5,4},{6,7},{7,6},{8,9},{9,8},{10,11... | collective-permute-start | bytes 2359304 | tf_op jit(solution)/shard_map/ppermute | solution.py:577
  82.0 33.7 %copy-start.38 = (bf16[768,1152]{1,0:T(8,128)(2,1)}, bf16[768,1152]{1,0:T(8,128)(2,1)S(1)}, u32[]{:S(2)}) copy-start(bf16[768,1152]{1,0:T(8,128)(2,1)S(1)} %fusion.40) | copy-start | bytes 5308420
  86.0 26.9 %copy-start.12 = (bf16[512,1152]{1,0:T(8,128)(2,1)}, bf16[512,1152]{1,0:T(8,128)(2,1)S(1)}, u32[]{:S(2)}) copy-start(bf16[512,1152]{1,0:T(8,128)(2,1)S(1)} %fusion.7.xp_ref) | copy-start | bytes 3538948
  113.0 35.8 %collective-permute-start.3 = (bf16[512,384]{1,0:T(8,128)(2,1)S(1)}, bf16[512,384]{1,0:T(8,128)(2,1)S(1)}, u32[]{:S(2)}, u32[]{:S(2)}) collective-permute-start(bf16[512,384]{1,0:T(8,128)(2,1)S(1)} %get-tuple-element.28.cp_ref), channel_id=1, source_target_pairs={{0,1},{1,0},{2,3},{3,2},{4,5},{5,4},{6,7},{7,6},{8,9},{9,8},{10,11... | collective-permute-start | bytes 1179656 | tf_op jit(solution)/shard_map/ppermute | solution.py:577
  118.5 27.7 %copy-start.8 = (bf16[512,1152]{1,0:T(8,128)(2,1)}, bf16[512,1152]{1,0:T(8,128)(2,1)S(1)}, u32[]{:S(2)}) copy-start(bf16[512,1152]{1,0:T(8,128)(2,1)S(1)} %fusion.5.xp_ref) | copy-start | bytes 3538948
  148.2 35.2 %copy-start.4 = (bf16[512,384]{1,0:T(8,128)(2,1)}, bf16[512,384]{1,0:T(8,128)(2,1)S(1)}, u32[]{:S(2)}) copy-start(bf16[512,384]{1,0:T(8,128)(2,1)S(1)} %get-tuple-element.25.cp_ref) | copy-start | bytes 1179652
  148.2 36.7 %collective-permute-start.1 = (bf16[512,384]{1,0:T(8,128)(2,1)S(1)}, bf16[512,384]{1,0:T(8,128)(2,1)S(1)}, u32[]{:S(2)}, u32[]{:S(2)}) collective-permute-start(bf16[512,384]{1,0:T(8,128)(2,1)S(1)} %get-tuple-element.25.cp_ref), channel_id=1, source_target_pairs={{0,1},{1,0},{2,3},{3,2},{4,5},{5,4},{6,7},{7,6},{8,9},{9,8},{10,11... | collective-permute-start | bytes 1179656 | tf_op jit(solution)/shard_map/ppermute | solution.py:577
  183.4 27.9 %collective-permute-start.6 = (bf16[512,384]{1,0:T(8,128)(2,1)}, bf16[512,384]{1,0:T(8,128)(2,1)S(1)}, u32[]{:S(2)}, u32[]{:S(2)}) collective-permute-start(bf16[512,384]{1,0:T(8,128)(2,1)} %get-tuple-element.38), channel_id=1, source_target_pairs={{0,1},{1,0},{2,3},{3,2},{4,5},{5,4},{6,7},{7,6},{8,9},{9,8},{10,11... | collective-permute-start | bytes 1179656 | tf_op jit(solution)/shard_map/ppermute | solution.py:577
  185.7 25.6 %copy-start.11 = (bf16[512,1152]{1,0:T(8,128)(2,1)S(1)}, bf16[512,1152]{1,0:T(8,128)(2,1)}, u32[]{:S(2)}) copy-start(bf16[512,1152]{1,0:T(8,128)(2,1)} %copy-done.10) | copy-start | bytes 3538948
  185.7 25.6 %copy-start.13 = (bf16[512,1152]{1,0:T(8,128)(2,1)S(1)}, bf16[512,1152]{1,0:T(8,128)(2,1)}, u32[]{:S(2)}) copy-start(bf16[512,1152]{1,0:T(8,128)(2,1)} %copy-done.12) | copy-start | bytes 3538948
  185.7 25.6 %copy-start.17 = (bf16[6,1024,128]{2,1,0:T(8,128)(2,1)S(1)}, bf16[6,1024,128]{2,1,0:T(8,128)(2,1)}, u32[]{:S(2)}) copy-start(bf16[6,1024,128]{2,1,0:T(8,128)(2,1)} %copy-done.16) | copy-start | bytes 4718596
  185.7 25.6 %copy-start.21 = (bf16[512,384]{1,0:T(8,128)(2,1)S(1)}, bf16[512,384]{1,0:T(8,128)(2,1)}, u32[]{:S(2)}) copy-start(bf16[512,384]{1,0:T(8,128)(2,1)} %copy-done.20) | copy-start | bytes 1179652
  185.7 25.6 %copy-start.23 = (bf16[512,384]{1,0:T(8,128)(2,1)S(1)}, bf16[512,384]{1,0:T(8,128)(2,1)}, u32[]{:S(2)}) copy-start(bf16[512,384]{1,0:T(8,128)(2,1)} %get-tuple-element.37.go_ref) | copy-start | bytes 1179652
  210.7 21.9 %collective-permute-start.4 = (bf16[512,384]{1,0:T(8,128)(2,1)}, bf16[512,384]{1,0:T(8,128)(2,1)S(1)}, u32[]{:S(2)}, u32[]{:S(2)}) collective-permute-start(bf16[512,384]{1,0:T(8,128)(2,1)} %get-tuple-element.32), channel_id=1, source_target_pairs={{0,1},{1,0},{2,3},{3,2},{4,5},{5,4},{6,7},{7,6},{8,9},{9,8},{10,11... | collective-permute-start | bytes 1179656 | tf_op jit(solution)/shard_map/ppermute | solution.py:577
  267.4 4.3 %collective-permute-start.8 = (f32[28,128]{1,0:T(8,128)S(1)}, f32[28,128]{1,0:T(8,128)S(1)}, u32[]{:S(2)}, u32[]{:S(2)}) collective-permute-start(f32[28,128]{1,0:T(8,128)S(1)} %maximum_bitcast_fusion), channel_id=1, source_target_pairs={{0,1},{1,0},{2,3},{3,2},{4,5},{5,4},{6,7},{7,6},{8,9},{9,8},{10,11... | collective-permute-start | bytes 43016 | tf_op jit(solution)/shard_map/ppermute | solution.py:577
  271.8 1.3 collective-permute-start.9
  273.1 4.2 %collective-permute-start.10 = (f32[28,128]{1,0:T(8,128)S(1)}, f32[28,128]{1,0:T(8,128)S(1)}, u32[]{:S(2)}, u32[]{:S(2)}) collective-permute-start(f32[28,128]{1,0:T(8,128)S(1)} %fusion.77), channel_id=1, source_target_pairs={{0,4},{2,6},{4,0},{6,2},{8,12},{10,14},{12,8},{14,10},{16,20},{18,... | collective-permute-start | bytes 43016 | tf_op jit(solution)/shard_map/ppermute | solution.py:584
  277.4 5.3 %collective-permute-start.11 = (f32[28,128]{1,0:T(8,128)S(1)}, f32[28,128]{1,0:T(8,128)S(1)}, u32[]{:S(2)}, u32[]{:S(2)}) collective-permute-start(f32[28,128]{1,0:T(8,128)S(1)} %add.128), channel_id=1, source_target_pairs={{0,8},{2,10},{4,12},{6,14},{8,0},{10,2},{12,4},{14,6},{16,24},{18,... | collective-permute-start | bytes 43016 | tf_op jit(solution)/shard_map/ppermute | solution.py:584
  282.0 20.5 %collective-permute-start.7 = (bf16[512,768]{1,0:T(8,128)(2,1)S(1)}, bf16[512,768]{1,0:T(8,128)(2,1)S(1)}, u32[]{:S(2)}, u32[]{:S(2)}) collective-permute-start(bf16[512,768]{1,0:T(8,128)(2,1)S(1)} %convolution_convert_fusion.4), channel_id=1, source_target_pairs={{0,1},{1,0},{2,3},{3,2},{4,5},{5,4},{6,7},{7,6},{8,9},{9,8},{10,11... | collective-permute-start | bytes 2359304 | tf_op jit(solution)/shard_map/ppermute | solution.py:577
  282.6 4.7 %collective-permute-start.12 = (f32[28,128]{1,0:T(8,128)S(1)}, f32[28,128]{1,0:T(8,128)S(1)}, u32[]{:S(2)}, u32[]{:S(2)}) collective-permute-start(f32[28,128]{1,0:T(8,128)S(1)} %add.129), channel_id=1, source_target_pairs={{0,16},{2,18},{4,20},{6,22},{8,24},{10,26},{12,28},{14,30},{16,0},... | collective-permute-start | bytes 43016 | tf_op jit(solution)/shard_map/ppermute | solution.py:584
  285.3 32.1 %collective-permute-start.5 = (bf16[512,768]{1,0:T(8,128)(2,1)S(1)}, bf16[512,768]{1,0:T(8,128)(2,1)S(1)}, u32[]{:S(2)}, u32[]{:S(2)}) collective-permute-start(bf16[512,768]{1,0:T(8,128)(2,1)S(1)} %convolution_convert_fusion.5), channel_id=1, source_target_pairs={{0,1},{1,0},{2,3},{3,2},{4,5},{5,4},{6,7},{7,6},{8,9},{9,8},{10,11... | collective-permute-start | bytes 2359304 | tf_op jit(solution)/shard_map/ppermute | solution.py:577
  (41 other events, 164.9 us)
Sparse Core Ops, SparseCore 0:
  16.4 53.1 all-gather.4
  71.8 87.2 all-gather.6
